TPU v7x, 256 devices: a whole 4x4x8 slice. The times are simulated.
256 devices in a mesh: row: 32 (over y, z), col: 8 (over x, core).
Axes of the slice: x: 4, y: 4, z: 8, core: 2. Of those that a mesh axis runs over, the one named last changes fastest.
Arguments:
- iterate: float32 [2048, 7168], P('row', 'col'), may hold values from -1 to 1
Outputs:
- update: float32 [2048, 7168], P('row', 'col')
All inputs are finite; a program needn't handle non-finite values.
Results may differ from a plain program's by a relative error of at most 0.00005.
Values sent between devices are 32-bit elements; how exact they have to be, the bound alone decides.
A program may use at most 64 MiB of HBM per device.

v0:
```python
import jax
import jax.numpy as jnp
from jax import lax
from jax.sharding import PartitionSpec as P

M = 2048
N = 7168


LINEAR_TERM = 3.4445
CUBIC_TERM = -4.775
QUINTIC_TERM = 2.0315
TARGET_SCALE = 0.2
EPSILON = 1e-07
PRECISE = lax.Precision.HIGHEST


def product(left, right):
    return jnp.dot(left, right, precision=PRECISE, preferred_element_type=jnp.float32)


def apply_rows(matrix, field):
    return product(matrix, lax.all_gather(field, "row", axis=0, tiled=True))


def body(iterate):
    gram_partial = product(iterate, lax.all_gather(iterate, "row", axis=0, tiled=True).T)
    gram_matrix = lax.psum(gram_partial, "col")
    applied_once = apply_rows(gram_matrix, iterate)
    applied_twice = apply_rows(gram_matrix, applied_once)
    polar_rows = LINEAR_TERM * iterate + (CUBIC_TERM * applied_once + QUINTIC_TERM * applied_twice)
    squares = lax.psum(jnp.sum(polar_rows * polar_rows), ("row", "col"))
    return TARGET_SCALE * polar_rows / jnp.sqrt(squares / (M * N) + EPSILON)


def solution(mesh):
    return jax.shard_map(
        body,
        mesh=mesh,
        in_specs=(P("row", "col"),),
        out_specs=P("row", "col"),
        check_vma=False,
    )
```

profile of v0, /device:TPU:1, one launch (start us, length us, event | category | flops | bytes accessed | tf_op | source)
XLA Modules:
  0.0 371.8 jit_solution(1522049066653344041)
XLA Ops:
  6.5 0.0 all-gather.3.cloned.1.call-start
  6.5 0.7 all-gather.3.cloned.1.call-update
  7.3 0.0 copy-start.1
  7.3 0.0 all-reduce.2.cloned.1.call-start
  7.3 99.4 %all-gather.3.cloned.1.call-done = f32[2048,896]{1,0:T(8,128)} async-done(((f32[64,896]{1,0:T(8,128)}), f32[2048,896]{1,0:T(8,128)}) %all-gather.3.cloned.1.call-update) | async-done | bytes 7340048 | tf_op jit(solution)/shard_map/all_gather | solution.py:27
  106.7 11.1 %fusion.2 = f32[64,2048]{1,0:T(8,128)} fusion(f32[64,896]{1,0:T(8,128)} %param.1, f32[2048,896]{1,0:T(8,128)} %all-gather.3.cloned.1.call-done), kind=kOutput, calls=%fused_computation.5 | convolution fusion | flops 1409286144 | bytes 8093696 | tf_op jit(solution)/shard_map/dot_general | solution.py:19
  117.8 0.0 all-reduce.2.cloned.1.call-update
  117.9 0.0 all-gather.5.cloned.1.call-start
  117.9 61.3 %all-reduce.2.cloned.1.call-done = f32[64,2048]{1,0:T(8,128)} async-done(((f32[64,2048]{1,0:T(8,128)}), f32[64,2048]{1,0:T(8,128)}) %all-reduce.2.cloned.1.call-update) | async-done | bytes 524304 | tf_op jit(solution)/shard_map/psum | solution.py:28
  179.2 0.0 copy-start
  179.2 8.2 %fusion.3 = f32[64,896]{1,0:T(8,128)} fusion(f32[64,2048]{1,0:T(8,128)} %all-reduce.2.cloned.1.call-done, f32[2048,896]{1,0:T(8,128)} %all-gather.3.cloned.1.call-done), kind=kOutput, calls=%fused_computation.6 | convolution fusion | flops 1409286144 | bytes 8093696 | tf_op jit(solution)/shard_map/dot_general | solution.py:19
  187.4 0.0 all-gather.5.cloned.1.call-update
  187.4 94.4 %all-gather.5.cloned.1.call-done = f32[2048,896]{1,0:T(8,128)} async-done(((f32[64,896]{1,0:T(8,128)}), f32[2048,896]{1,0:T(8,128)}) %all-gather.5.cloned.1.call-update) | async-done | bytes 7340048 | tf_op jit(solution)/shard_map/all_gather | solution.py:23
  281.8 0.0 copy-done.1
  281.8 0.0 copy-done
  281.8 7.2 %multiply_reduce_fusion = (f32[]{:T(128)}, f32[64,896]{1,0:T(8,128)S(1)}) fusion(f32[64,2048]{1,0:T(8,128)S(1)} %copy-done, f32[2048,896]{1,0:T(8,128)} %all-gather.5.cloned.1.call-done, f32[64,896]{1,0:T(8,128)} %fusion.3, f32[64,896]{1,0:T(8,128)S(1)} %copy-done.1), kind=kOutput, calls=%fused_computation.3 | convolution fusion | flops 1409687552 | bytes 8552452 | tf_op jit(solution)/shard_map/dot_general | solution.py:19
  288.9 75.0 %psum.15 = f32[]{:T(128)} all-reduce(f32[]{:T(128)} %get-tuple-element.5), channel_id=1, replica_groups=mesh['row'=32,'col'=8] {'row','col'}, use_global_device_ids=true, to_apply=%region_2.0 | all-reduce | flops 1 | bytes 8 | tf_op jit(solution)/shard_map/psum | solution.py:32
  364.6 0.7 multiply_divide_fusion
Async XLA Ops:
  6.5 100.2 %all-gather.3.cloned.1.call-start = ((), (), s32[]{:S(2)}) async-start(), calls=%async_computation | async-start | bytes 7569408 | tf_op jit(solution)/shard_map/all_gather | solution.py:27
  7.3 274.5 %copy-start.1 = (f32[64,896]{1,0:T(8,128)S(1)}, f32[64,896]{1,0:T(8,128)}, u32[]{:S(2)}) copy-start(f32[64,896]{1,0:T(8,128)} %param.1) | copy-start | bytes 688132
  7.3 171.9 %all-reduce.2.cloned.1.call-start = ((), (), s32[]{:S(2)}) async-start(), calls=%async_computation.1 | async-start | bytes 1048576 | tf_op jit(solution)/shard_map/psum | solution.py:28
  117.9 163.9 %all-gather.5.cloned.1.call-start = ((), (), s32[]{:S(2)}) async-start(), calls=%async_computation.2 | async-start | bytes 7569408 | tf_op jit(solution)/shard_map/all_gather | solution.py:23
  179.2 102.6 %copy-start = (f32[64,2048]{1,0:T(8,128)S(1)}, f32[64,2048]{1,0:T(8,128)}, u32[]{:S(2)}) copy-start(f32[64,2048]{1,0:T(8,128)} %all-reduce.2.cloned.1.call-done) | copy-start | bytes 1572868
Sparse Core Ops, SparseCore 0:
  9.9 96.7 all-gather.2
  118.0 61.1 all-reduce.1
  187.5 94.1 all-gather.4
where the time goes:
time: 372 us
  waiting for transfers between devices  256 us (69%)
  blocking collectives  75 us (20%)
  matrix products  26.5 us (7%)
  between operations  13.8 us (4%)
    all_gather x1, waiting for transfers between devices, body(): lax.all_gather(iterate, 'row', axis=0, tiled=True)  99.4 us
    all_gather x1, waiting for transfers between devices, apply_rows(): return product(matrix, lax.all_gather(field, 'row', axis=0, tiled=True))  94.4 us
    psum x1, blocking collectives, body(): squares = lax.psum(jnp.sum(polar_rows * polar_rows), ('row', 'col'))  75 us
    psum x1, waiting for transfers between devices, body(): gram_matrix = lax.psum(gram_partial, 'col')  61.3 us
    dot_general x3, matrix products, product(): jnp.dot(left, right, precision=PRECISE, preferred_element_type=jnp.float32)  26.5 us
  transfers between devices with their start and end apart: 3, of which 3 were waited for; matrix products, arithmetic and copies ran while one was open for 0% of the time, Pallas kernels for 0%

commit v1 on v0

v1 whole, which is shorter than its diff:
```python
import functools
import jax
import jax.numpy as jnp
from jax import lax
from jax.experimental import pallas as pl
from jax.experimental.pallas import tpu as pltpu
from jax.sharding import PartitionSpec as P

M = 2048
N = 7168
NY = 4
NZ = 8
X_PARTS = 4

LINEAR_TERM = 3.4445
CUBIC_TERM = -4.775
QUINTIC_TERM = 2.0315
TARGET_SCALE = 0.2
EPSILON = 1e-07
MESH = pl.DeviceIdType.MESH
F32 = jnp.float32
BF16 = jnp.bfloat16


def split(value):
    high = value.astype(BF16)
    return high, (value - high.astype(F32)).astype(BF16)


def dot3(left, right, left_dim, right_dim):
    return lax.dot_general(
        jnp.concatenate([left[0], left[0], left[1]], axis=left_dim),
        jnp.concatenate([right[0], right[1], right[0]], axis=right_dim),
        (((left_dim,), (right_dim,)), ((), ())),
        preferred_element_type=F32,
    )


class Ring:
    def __init__(self, n, parts, device, src, land, two, every, send_sem, recv_sem):
        self.parts, self.device, self.src, self.land = parts, device, src, land
        self.two, self.every, self.send_sem, self.recv_sem = two, every, send_sem, recv_sem
        self.items = ring_items(n, parts)

    def copy(self, src, dst, t, way):
        return pltpu.make_async_remote_copy(
            src_ref=src,
            dst_ref=dst,
            send_sem=self.send_sem,
            recv_sem=self.recv_sem.at[t],
            device_id=self.device(way),
            device_id_type=MESH,
        )

    def send(self, t):
        for way in (1, -1):
            d, h = t // self.parts, t % self.parts
            h = h if way > 0 else self.parts - 1 - h
            self.copy(self.src(way, d, h), self.land(way, d, h), t, way).start()

    def open(self):
        for t in range(min(self.parts, self.items)):
            self.send(t)

    def take(self, t):
        self.copy(self.two, self.two, t, 1).wait_recv()
        if t + self.parts < self.items:
            self.send(t + self.parts)

    def close(self):
        self.copy(self.every, self.every, 0, 1).wait_send()


def ring_items(n, parts):
    return parts * (n - 1) // 2


def slot_order(n):
    out = [0]
    for s in range(1, n // 2):
        out += [s, n - s]
    return out + [n // 2]


def kernel(
    nc, x_hbm, out_ref,
    xv, xz, xy, xhi, xlo, jhi, jlo, gp, gr, gs, gy, gj, tt, tz, thi, tlo, cp, cr, pp, qy, qk, pthi, ptlo, op, ry,
    sq, sqx, sqz, sqy,
    x_s, xz_s, xz_r, xy_s, xy_r, g_s, g_r, gy_s, gy_r, tz_s, tz_r, c_s, c_r, u_s, u_r, v_s, v_r, p_s, p_r, qk_s, qk_r, ry_s, ry_r,
    qx_s, qx_r, qz_s, qz_r, qy_s, qy_r,
):
    rows, width = xv.shape
    half = rows // 2
    sub = rows // nc
    owned = NZ * sub
    wide = NY * rows
    row, col = lax.axis_index("row"), lax.axis_index("col")
    y, z = lax.div(row, NZ), lax.rem(row, NZ)

    def at_y(step):
        return (lax.rem(y + step + NY, NY) * NZ + z, col)

    def at_z(step):
        return (y * NZ + lax.rem(z + step + NZ, NZ), col)

    nx = nc // 2
    x, core = lax.div(col, 2), lax.rem(col, 2)
    twin = (row, col + 1 - 2 * core)

    def at_x(step):
        return (row, lax.rem(x + step + nx, nx) * 2 + core)

    def at_col(step):
        return (row, lax.rem(col + step, nc))

    def copy(src, dst, send_sem, recv_sem, device):
        return pltpu.make_async_remote_copy(
            src_ref=src, dst_ref=dst, send_sem=send_sem, recv_sem=recv_sem, device_id=device, device_id_type=MESH
        )

    fetch = pltpu.make_async_copy(x_hbm, xv, x_s)
    fetch.start()
    barrier = pltpu.get_barrier_semaphore()
    friends = [at_z(1), at_z(-1), at_y(1), at_y(-1), at_y(2)]
    friends += [at_z(s) for s in range(2, NZ - 1)] + [at_col(s) for s in range(1, nc)]
    for friend in friends:
        pl.semaphore_signal(barrier, inc=1, device_id=friend, device_id_type=MESH)
    pl.semaphore_wait(barrier, len(friends))

    def halves(h):
        return pl.ds(h * half, half)

    def block_ring(n, parts, device, own, buf, send_sem, recv_sem):
        def src(way, d, h):
            return own(h) if d == 0 else buf.at[way * d % n, pl.ds(h * (rows // parts), rows // parts)]

        def land(way, d, h):
            return buf.at[way * (d + 1) % n, pl.ds(h * (rows // parts), rows // parts)]

        two = buf.at[0, pl.ds(0, 2 * (rows // parts))]
        return Ring(n, parts, device, src, land, two, buf.at[pl.ds(0, n - 1)], send_sem, recv_sem)

    def own_x(h):
        return x_hbm.at[pl.ds(h * (rows // X_PARTS), rows // X_PARTS)]

    z_ring = block_ring(NZ, X_PARTS, at_z, own_x, xz, xz_s, xz_r)
    y_ring = block_ring(NY, X_PARTS, at_y, own_x, xy, xy_s, xy_r)
    z_ring.open()
    y_ring.open()
    fetch.wait()
    order = slot_order(NZ)
    closing = []

    def span(first, last):
        return pl.ds(first * rows, (last - first) * rows)

    def keep_j(slot, value):
        where = pl.ds(pl.multiple_of(lax.rem(y - slot + NY, NY) * rows, rows), rows)
        hi, lo = split(value)
        jhi[where, :] = hi
        jlo[where, :] = lo

    def keep_i(pos, value):
        hi, lo = split(value)
        xhi[span(pos, pos + 1), :] = hi
        xlo[span(pos, pos + 1), :] = lo

    def each(n, act):
        for j in sorted(range(1, n), key=lambda j: -min(j, n - j)):
            act(j)

    def fan(n, whole, send_sem, recv_sem, make):
        every = copy(whole, whole, send_sem, recv_sem, twin)
        each(n, lambda j: copy(*make(j)[:2], send_sem, recv_sem, make(j)[2]).start())
        closing.append(every.wait_send)
        return every.wait_recv

    def scatter(part, buf, b, first, last, send_sem, recv_sem):
        def make(j):
            to = at_col(j)
            mine_there = pl.ds(pl.multiple_of(to[1] * sub, sub), sub)
            return part.at[pl.ds(first, last - first), mine_there], buf.at[j - 1, pl.ds(first, last - first)], to

        return fan(nc, buf.at[:, pl.ds(first, last - first)], send_sem.at[b], recv_sem.at[b], make)

    def gathered(part, buf, pos):
        total = part[pos, pl.ds(pl.multiple_of(col * sub, sub), sub), :]
        for j in range(1, nc):
            total = total + buf[j - 1, pos]
        return total

    def spread_y(src, buf, b, first, last, send_sem, recv_sem):
        where = pl.ds(first, last - first)
        return fan(
            NY, buf.at[:, where], send_sem.at[b], recv_sem.at[b], lambda s: (src, buf.at[s - 1, where], at_y(s))
        )

    keep_i(0, xv[...])
    keep_j(0, xv[...])
    y_waits, arrivals = [], []
    spans = ((0, 5), (5, NZ))

    def gram(first, last):
        for pos in range(first, last):
            if pos:
                keep_i(pos, xz[order[pos]])
        where = span(first, last)
        block = dot3((xhi[where, :], xlo[where, :]), (jhi[...], jlo[...]), 1, 1)
        gp[first:last] = block.reshape(last - first, rows, wide)

    y_spans = ((0, 4), (4, 7), (7, NZ))

    def drain_g(b, which):
        first, last = y_spans[b]
        for one in which:
            arrivals[one]()
        for pos in range(first, last):
            gs[pos] = gathered(gp, gr, pos)
        y_waits.append(spread_y(gs.at[pl.ds(first, last - first)], gy, b, first, last, gy_s, gy_r))

    for item in range(z_ring.items):
        z_ring.take(item)
        if item < y_ring.items:
            y_ring.take(item)
        t = (2 * item + 2) / X_PARTS - 1
        if t == 1:
            keep_j(1, xy[1])
            keep_j(NY - 1, xy[NY - 1])
        if t == 2:
            keep_j(2, xy[2])
            gram(0, 3)
            arrivals.append(scatter(gp, gr, 0, 0, 3, g_s, g_r))
        if t == 3:
            gram(3, 4)
            arrivals.append(scatter(gp, gr, 1, 3, 4, g_s, g_r))
        if t == 4:
            gram(4, 5)
            arrivals.append(scatter(gp, gr, 2, 4, 5, g_s, g_r))
        if t == 5:
            gram(5, 7)
            arrivals.append(scatter(gp, gr, 3, 5, 7, g_s, g_r))
            drain_g(0, (0, 1))
        if t == 6:
            gram(7, NZ)
            arrivals.append(scatter(gp, gr, 4, 7, NZ, g_s, g_r))
            drain_g(1, (2, 3))

    group = NY * sub

    def place(slot, pos):
        first = (order[pos] + 1) % NZ * group
        return pl.ds(pl.multiple_of(first + lax.rem(y - slot + NY, NY) * sub, sub), sub)

    def settle(b):
        first, last = y_spans[b]
        for pos in range(first, last):
            gj[place(0, pos), :] = gs[pos]
        y_waits[b]()
        for slot in range(1, NY):
            for pos in range(first, last):
                gj[place(slot, pos), :] = gy[slot - 1, pos]

    mine = pl.ds(pl.multiple_of(y * rows, rows), rows)
    lanes = owned * NY // 2
    near = [(0, 1, 1, 0, rows), (0, -1, NZ - 1, 0, rows)]
    last = [(2, 2, 4, 0, half), (NZ - 2, -2, 4, half, half)]
    t_moves = (
        near + [(1, 1, 2, 0, rows), (NZ - 1, -1, NZ - 2, 0, rows), (2, 1, 3, 0, rows), (NZ - 2, -1, NZ - 3, 0, rows)] + last,
        near + [(0, 2, 2, 0, rows), (0, -2, NZ - 2, 0, rows), (1, 2, 3, 0, rows), (NZ - 1, -2, NZ - 3, 0, rows)] + last,
    )

    def t_copy(part, k, src, dst):
        return copy(src, dst, tz_s.at[part], tz_r.at[part, k // 2], at_z(t_moves[part][k][1]))

    def t_start(part, first):
        for k in range(first, first + 2):
            source, _, slot, start, size = t_moves[part][k]
            own = tt.at[part, pl.ds(pl.multiple_of(y * rows + start, half), size)]
            src = tz.at[part, source, pl.ds(start, size)] if source else own
            t_copy(part, k, src, tz.at[part, slot, pl.ds(start, size)]).start()

    def t_wait(part, first):
        two = tz.at[part, pl.ds(0, 2 if first < 6 else 1)]
        t_copy(part, first, two, two).wait_recv()

    def t_open(part):
        tt[part] = gj[pl.ds(part * lanes, lanes), :].T
        t_start(part, 0)

    settle(0)
    t_open(0)
    drain_g(2, (4,))
    z_ring.close()
    t_wait(0, 0)
    t_start(0, 2)
    settle(1)
    settle(2)
    t_open(1)
    t_start(1, 2)
    t_wait(0, 2)
    t_start(0, 4)
    t_start(0, 6)

    right = split(gj[...])
    k_waits, arrivals = [], []

    def square(first, last):
        for pos in range(first, last):
            slot = order[pos]
            halves_t = [tz[part, slot] if pos else tt[part, mine, :] for part in range(2)]
            whole = jnp.concatenate(halves_t, axis=1)
            hi, lo = split(pltpu.roll(whole, slot * group, 1) if pos else whole)
            thi[span(pos, pos + 1), :] = hi
            tlo[span(pos, pos + 1), :] = lo
        where = span(first, last)
        block = dot3((thi[where, :], tlo[where, :]), right, 1, 0)
        cp[first:last] = block.reshape(last - first, rows, wide)

    def drain_c(first, last, which):
        for one in which:
            arrivals[one]()
        for pos in range(first, last):
            value = CUBIC_TERM * gs[pos] + QUINTIC_TERM * gathered(cp, cr, pos)
            if pos == 0:
                lane = lax.broadcasted_iota(jnp.int32, value.shape, 1)
                diagonal = lax.broadcasted_iota(jnp.int32, value.shape, 0) + (y * rows + col * sub)
                value = value + jnp.where(lane == diagonal, LINEAR_TERM, 0.0)
            pp[pos, x, core] = value

    first_span = pl.ds(0, spans[0][1])
    u_every = pp.at[first_span, pl.ds(0, nx - 1), core]
    u_all = copy(u_every, u_every, u_s, u_r, twin)
    v_mine, v_there = pp.at[first_span, :, core], pp.at[first_span, :, 1 - core]
    to_twin, from_twin = copy(v_mine, v_mine, v_s, v_r, twin), copy(v_there, v_there, v_s, v_r, twin)

    def to_chips():
        part = pp.at[first_span, x, core]
        for j in (2, 1, 3):
            copy(part, part, u_s, u_r, at_x(j)).start()

    def to_all(b, first, last):
        part = pp.at[pl.ds(first, last - first), x, core]
        every = pp.at[pl.ds(0, nc - 1), pl.ds(0, last - first), 0]
        return fan(nc, every, p_s.at[b], p_r.at[b], lambda j: (part, part, at_col(j)))

    old = closing[:]
    closing.clear()
    square(0, 1)
    arrivals.append(scatter(cp, cr, 0, 0, 1, c_s, c_r))
    y_ring.close()
    for done in old:
        done()
    for b in range(1, 3):
        t_wait(1, 2 * b - 2)
        t_start(1, 2 * b + 2)
        square(2 * b - 1, 2 * b + 1)
        arrivals.append(scatter(cp, cr, b, 2 * b - 1, 2 * b + 1, c_s, c_r))
    t_wait(0, 4)
    t_wait(1, 4)
    square(5, 7)
    arrivals.append(scatter(cp, cr, 3, 5, 7, c_s, c_r))
    t_wait(0, 6)
    t_wait(1, 6)
    square(7, NZ)
    arrivals.append(scatter(cp, cr, 4, 7, NZ, c_s, c_r))
    drain_c(0, 5, (0, 1, 2))
    to_chips()
    drain_c(5, 7, (3,))
    from_all = [to_all(0, 5, 7)]
    drain_c(7, NZ, (4,))
    from_all.append(to_all(1, 7, NZ))
    for b, (first, last) in enumerate(spans):
        k_waits.append(spread_y(pp.at[pl.ds(first, last - first), x, core], qy, b, first, last, qk_s, qk_r))
    u_all.wait_recv()
    to_twin.start()
    for half_t in range(2):
        every = tz.at[half_t, pl.ds(0, NZ - 1)]
        t_copy(half_t, 0, every, every).wait_send()

    cut = (width // 128 + 1) // 2 * 128
    parts = (pl.ds(0, cut), pl.ds(cut, width - cut))
    most = NZ // 2
    early = most * rows
    from_twin.wait_recv()
    known = jnp.concatenate([pp[:most].reshape(early, wide), jnp.zeros((NZ * rows - early, wide), F32)], axis=0)
    hi, lo = split(known.T)
    pthi[...] = hi
    ptlo[...] = lo
    for c in range(2):
        block = dot3((pthi[...], ptlo[...]), (xhi[:, parts[c]], xlo[:, parts[c]]), 1, 0)
        op[:, :, parts[c]] = block.reshape(NY, rows, block.shape[-1])
    from_all[0]()
    from_all[1]()
    late = split(pp[most:].reshape(NZ * rows - early, wide).T)

    def product(c):
        block = dot3(late, (xhi[early:, parts[c]], xlo[early:, parts[c]]), 1, 0)
        op[:, :, parts[c]] = op[:, :, parts[c]] + block.reshape(NY, rows, block.shape[-1])

    def pass_on(way, t, step, h, c):
        w = 0 if way > 0 else 1
        part = op.at[lax.rem(y + way * step + NY, NY), halves(h), parts[c]]
        copy(part, ry.at[w, t, :, parts[c]], ry_s.at[c], ry_r.at[min(t, 1), c], at_y(way)).start()

    def arrived(kind, c):
        here = ry.at[:, 1:3, :, parts[c]] if kind else ry.at[:, 0, :, parts[c]]
        copy(here, here, ry_s.at[c], ry_r.at[kind, c], at_y(1)).wait_recv()

    def begin(c):
        product(c)
        for way in (1, -1):
            pass_on(way, 0, 2, 0 if way > 0 else 1, c)
        for way in (1, -1):
            pass_on(way, 1, 1, 1 if way > 0 else 0, c)

    def finish(c):
        arrived(0, c)
        for way in (1, -1):
            w = h = 0 if way > 0 else 1
            to = lax.rem(y + way + NY, NY)
            op[to, halves(h), parts[c]] = op[to, halves(h), parts[c]] + ry[w, 0, :, parts[c]]
            pass_on(way, 2, 1, h, c)

    def squares_here():
        for pos in range(NZ):
            qk[place(0, pos), :] = pp[pos, x, core]
        for arrive in k_waits:
            arrive()
        for slot in range(1, NY):
            for pos in range(NZ):
                qk[place(slot, pos), :] = qy[slot - 1, pos]
        block = dot3((thi[...], tlo[...]), split(qk[...]), 1, 0)
        block = block * pp[...].reshape(NZ * rows, wide)
        columns = jnp.sum(block.reshape(NZ * rows // 8, 8, wide), axis=0)
        total = columns[:, :128]
        for c in range(1, wide // 128):
            total = total + columns[:, c * 128 : (c + 1) * 128]
        return total

    stages = ((nc, at_col, sqx, qx_s, qx_r), (NZ, at_z, sqz, qz_s, qz_r), (NY, at_y, sqy, qy_s, qy_r))

    def give(stage, total):
        n, device, buf, send_sem, recv_sem = stages[stage]
        sq[stage] = total
        return fan(n, buf, send_sem, recv_sem, lambda s: (sq.at[stage], buf.at[s - 1], device(s)))

    def take(stage, now, total):
        now()
        for one in range(stages[stage][0] - 1):
            total = total + stages[stage][2][one]
        return total

    begin(0)
    total = squares_here()
    now = give(0, total)
    begin(1)
    total = take(0, now, total)
    now = give(1, total)
    finish(0)
    finish(1)
    total = take(1, now, total)
    now = give(2, total)
    for done in closing[:-1]:
        done()
    total = take(2, now, total)
    squares = jnp.sum(jnp.sum(total, axis=1, keepdims=True), axis=0, keepdims=True)
    factor = TARGET_SCALE / jnp.sqrt(squares / (M * N) + EPSILON)

    u_all.wait_send()
    to_twin.wait_send()
    arrived(1, 0)
    arrived(1, 1)
    for h in range(2):
        total = op[y, halves(h), :] + (ry[0, 2 - h, :, :] + ry[1, 1 + h, :, :])
        out_ref[halves(h), :] = factor * total
    for c in range(2):
        every = ry.at[:, :, :, parts[c]]
        copy(every, every, ry_s.at[c], ry_r.at[0, c], at_y(1)).wait_send()
    closing[-1]()


def body(nc, iterate):
    rows, width = iterate.shape
    sub = rows // nc
    wide = NY * rows
    owned = NY * NZ * sub
    vmem = pltpu.VMEM
    dma = pltpu.SemaphoreType.DMA

    def pair(*shape):
        return [dma(shape), dma(shape)]

    return pl.pallas_call(
        functools.partial(kernel, nc),
        out_shape=vmem((rows, width), F32),
        in_specs=[pl.BlockSpec(memory_space=pl.ANY)],
        out_specs=pl.BlockSpec(memory_space=vmem),
        scratch_shapes=[
            vmem((rows, width), F32),
            vmem((NZ, rows, width), F32),
            vmem((NY, rows, width), F32),
            vmem((NZ * rows, width), BF16),
            vmem((NZ * rows, width), BF16),
            vmem((wide, width), BF16),
            vmem((wide, width), BF16),
            vmem((NZ, rows, wide), F32),
            vmem((nc - 1, NZ, sub, wide), F32),
            vmem((NZ, sub, wide), F32),
            vmem((NY - 1, NZ, sub, wide), F32),
            vmem((owned, wide), F32),
            vmem((2, wide, owned // 2), F32),
            vmem((2, NZ, rows, owned // 2), F32),
            vmem((NZ * rows, owned), BF16),
            vmem((NZ * rows, owned), BF16),
            vmem((NZ, rows, wide), F32),
            vmem((nc - 1, NZ, sub, wide), F32),
            vmem((NZ, nc // 2, 2, sub, wide), F32),
            vmem((NY - 1, NZ, sub, wide), F32),
            vmem((owned, wide), F32),
            vmem((wide, NZ * rows), BF16),
            vmem((wide, NZ * rows), BF16),
            vmem((NY, rows, width), F32),
            vmem((2, 3, rows // 2, width), F32),
            vmem((3, 8, 128), F32),
            vmem((nc - 1, 8, 128), F32),
            vmem((NZ - 1, 8, 128), F32),
            vmem((NY - 1, 8, 128), F32),
            dma,
        ]
        + [dma, dma((ring_items(NZ, X_PARTS),))]
        + [dma, dma((ring_items(NY, X_PARTS),))]
        + pair(5)
        + pair(3)
        + [dma((2,)), dma((2, 4))]
        + pair(5)
        + [dma] * 4
        + pair(2)
        + pair(2)
        + [dma((2,)), dma((2, 2))]
        + [dma] * 6,
        compiler_params=pltpu.CompilerParams(
            collective_id=0, has_side_effects=True, vmem_limit_bytes=56 * 1024 * 1024
        ),
    )(iterate)


def solution(mesh):
    return jax.shard_map(
        functools.partial(body, mesh.shape["col"]),
        mesh=mesh,
        in_specs=(P("row", "col"),),
        out_specs=P("row", "col"),
        check_vma=False,
    )
```

time: 372 us -> 68.4 us (0.18)
  waiting for transfers between devices: 256 us -> 0 us
  blocking collectives: 75 us -> 0 us
  Pallas kernels: 0 us -> 67.4 us
  matrix products: 26.5 us -> 0 us
  between operations: 13.8 us -> 0.01 us
    all_gather x2 -> x0, waiting for transfers between devices: 194 us -> none  [the longest x1 99.4 us: body(): lax.all_gather(iterate, 'row', axis=0, tiled=True)]
    psum x1 -> x0, blocking collectives: 75 us -> none  [body(): squares = lax.psum(jnp.sum(polar_rows * polar_rows), ('row', 'col'))]
    pallas_call x0 -> x1, Pallas kernels: none -> 67.4 us  [body(): pl.pallas_call(functools.partial(kernel, nc), out_shape=vmem((rows, width...]
    psum x1 -> x0, waiting for transfers between devices: 61.3 us -> none  [body(): gram_matrix = lax.psum(gram_partial, 'col')]
    dot_general x3 -> x0, matrix products: 26.5 us -> none  [product(): jnp.dot(left, right, precision=PRECISE, preferred_element_type=jnp.float32)]
  transfers between devices with their start and end apart: 3 -> 0, of which waited for: 3 -> 0; matrix products, arithmetic and copies ran while one was open for 0% -> 0% of each run, Pallas kernels for 0% -> 0%
where the time goes in v1:
time: 68.4 us; the launch traced here: 68.1 us
  Pallas kernels  67.4 us (99%)
  local copies, waits for them, and re-layouts  0.69 us (1%)
    pallas_call x1, Pallas kernels, body(): pl.pallas_call(functools.partial(kernel, nc), out_shape=vmem((rows, width...  67.4 us

profile of v1, /device:TPU:1, one launch (start us, length us, event | category | flops | bytes accessed | tf_op | source)
XLA Modules:
  0.0 68.1 jit_solution(2784613788865723907)
XLA Ops:
  0.0 67.4 %shard_map.17 = f32[64,896]{1,0:T(8,128)S(1)} custom-call(f32[64,896]{1,0:T(8,128)} %x_hbm.1), custom_call_target="tpu_custom_call" | custom-call | tf_op jit(solution)/shard_map/pallas_call | solution.py:493
  67.5 0.7 %copy.3 = f32[64,896]{1,0:T(8,128)} copy(f32[64,896]{1,0:T(8,128)S(1)} %shard_map.17) | data formatting | bytes 458752

commit v2 on v1

--- a/solution.py
+++ b/solution.py
@@ -236,14 +236,13 @@
         if t == 4:
             gram(4, 5)
             arrivals.append(scatter(gp, gr, 2, 4, 5, g_s, g_r))
+            drain_g(0, (0, 1))
         if t == 5:
             gram(5, 7)
             arrivals.append(scatter(gp, gr, 3, 5, 7, g_s, g_r))
-            drain_g(0, (0, 1))
         if t == 6:
             gram(7, NZ)
             arrivals.append(scatter(gp, gr, 4, 7, NZ, g_s, g_r))
-            drain_g(1, (2, 3))
 
     group = NY * sub
 
@@ -260,7 +259,8 @@
             for pos in range(first, last):
                 gj[place(slot, pos), :] = gy[slot - 1, pos]
 
-    mine = pl.ds(pl.multiple_of(y * rows, rows), rows)
+    pair_of_y, in_pair = lax.div(y, 2), lax.rem(y, 2)
+    mine = pl.ds(pl.multiple_of(in_pair * rows, rows), rows)
     lanes = owned * NY // 2
     near = [(0, 1, 1, 0, rows), (0, -1, NZ - 1, 0, rows)]
     last = [(2, 2, 4, 0, half), (NZ - 2, -2, 4, half, half)]
@@ -275,7 +275,7 @@
     def t_start(part, first):
         for k in range(first, first + 2):
             source, _, slot, start, size = t_moves[part][k]
-            own = tt.at[part, pl.ds(pl.multiple_of(y * rows + start, half), size)]
+            own = tt.at[part, pl.ds(pl.multiple_of(in_pair * rows + start, half), size)]
             src = tz.at[part, source, pl.ds(start, size)] if source else own
             t_copy(part, k, src, tz.at[part, slot, pl.ds(start, size)]).start()
 
@@ -284,11 +284,13 @@
         t_copy(part, first, two, two).wait_recv()
 
     def t_open(part):
-        tt[part] = gj[pl.ds(part * lanes, lanes), :].T
+        columns = pl.ds(pl.multiple_of(pair_of_y * 2 * rows, 2 * rows), 2 * rows)
+        tt[part] = gj[pl.ds(part * lanes, lanes), columns].T
         t_start(part, 0)
 
     settle(0)
     t_open(0)
+    drain_g(1, (2, 3))
     drain_g(2, (4,))
     z_ring.close()
     t_wait(0, 0)
@@ -363,21 +365,26 @@
     t_wait(1, 6)
     square(7, NZ)
     arrivals.append(scatter(cp, cr, 4, 7, NZ, c_s, c_r))
+
+    def rows_to_y(b, first, last):
+        k_waits.append(spread_y(pp.at[pl.ds(first, last - first), x, core], qy, b, first, last, qk_s, qk_r))
+
     drain_c(0, 5, (0, 1, 2))
     to_chips()
+    rows_to_y(0, 0, 5)
     drain_c(5, 7, (3,))
     from_all = [to_all(0, 5, 7)]
     drain_c(7, NZ, (4,))
     from_all.append(to_all(1, 7, NZ))
-    for b, (first, last) in enumerate(spans):
-        k_waits.append(spread_y(pp.at[pl.ds(first, last - first), x, core], qy, b, first, last, qk_s, qk_r))
+    rows_to_y(1, 5, 7)
+    rows_to_y(2, 7, NZ)
     u_all.wait_recv()
     to_twin.start()
     for half_t in range(2):
         every = tz.at[half_t, pl.ds(0, NZ - 1)]
         t_copy(half_t, 0, every, every).wait_send()
 
-    cut = (width // 128 + 1) // 2 * 128
+    cut = width - 256
     parts = (pl.ds(0, cut), pl.ds(cut, width - cut))
     most = NZ // 2
     early = most * rows
@@ -508,7 +515,7 @@
             vmem((NZ, sub, wide), F32),
             vmem((NY - 1, NZ, sub, wide), F32),
             vmem((owned, wide), F32),
-            vmem((2, wide, owned // 2), F32),
+            vmem((2, 2 * rows, owned // 2), F32),
             vmem((2, NZ, rows, owned // 2), F32),
             vmem((NZ * rows, owned), BF16),
             vmem((NZ * rows, owned), BF16),
@@ -535,7 +542,7 @@
         + pair(5)
         + [dma] * 4
         + pair(2)
-        + pair(2)
+        + pair(3)
         + [dma((2,)), dma((2, 2))]
         + [dma] * 6,
         compiler_params=pltpu.CompilerParams(

time: 68.4 us -> 67.6 us (0.988)
  no operation moved by 1% of the time
where the time goes in v2:
time: 67.6 us
  Pallas kernels  66.9 us (99%)
  local copies, waits for them, and re-layouts  0.69 us (1%)
    pallas_call x1, Pallas kernels, body(): pl.pallas_call(functools.partial(kernel, nc), out_shape=vmem((rows, width...  66.9 us

profile of v2, /device:TPU:1, one launch (start us, length us, event | category | flops | bytes accessed | tf_op | source)
XLA Modules:
  0.0 67.6 jit_solution(18262313087009455969)
XLA Ops:
  0.0 66.9 %shard_map.17 = f32[64,896]{1,0:T(8,128)S(1)} custom-call(f32[64,896]{1,0:T(8,128)} %x_hbm.1), custom_call_target="tpu_custom_call" | custom-call | tf_op jit(solution)/shard_map/pallas_call | solution.py:500
  66.9 0.7 %copy.3 = f32[64,896]{1,0:T(8,128)} copy(f32[64,896]{1,0:T(8,128)S(1)} %shard_map.17) | data formatting | bytes 458752

commit v3 on v2

--- a/solution.py
+++ b/solution.py
@@ -266,7 +266,7 @@
     last = [(2, 2, 4, 0, half), (NZ - 2, -2, 4, half, half)]
     t_moves = (
         near + [(1, 1, 2, 0, rows), (NZ - 1, -1, NZ - 2, 0, rows), (2, 1, 3, 0, rows), (NZ - 2, -1, NZ - 3, 0, rows)] + last,
-        near + [(0, 2, 2, 0, rows), (0, -2, NZ - 2, 0, rows), (1, 2, 3, 0, rows), (NZ - 1, -2, NZ - 3, 0, rows)] + last,
+        near + [(0, 2, 2, 0, rows), (0, -2, NZ - 2, 0, rows), (2, 1, 3, 0, rows), (NZ - 2, -1, NZ - 3, 0, rows)] + last,
     )
 
     def t_copy(part, k, src, dst):
@@ -352,9 +352,11 @@
     y_ring.close()
     for done in old:
         done()
+    t_wait(1, 0)
+    t_wait(1, 2)
+    t_start(1, 4)
+    t_start(1, 6)
     for b in range(1, 3):
-        t_wait(1, 2 * b - 2)
-        t_start(1, 2 * b + 2)
         square(2 * b - 1, 2 * b + 1)
         arrivals.append(scatter(cp, cr, b, 2 * b - 1, 2 * b + 1, c_s, c_r))
     t_wait(0, 4)
@@ -374,9 +376,9 @@
     rows_to_y(0, 0, 5)
     drain_c(5, 7, (3,))
     from_all = [to_all(0, 5, 7)]
+    rows_to_y(1, 5, 7)
     drain_c(7, NZ, (4,))
     from_all.append(to_all(1, 7, NZ))
-    rows_to_y(1, 5, 7)
     rows_to_y(2, 7, NZ)
     u_all.wait_recv()
     to_twin.start()

time: 67.6 us -> 67.4 us (level)
  no operation moved by 1% of the time
where the time goes in v3:
time: 67.4 us; the launch traced here: 67.3 us
  Pallas kernels  66.6 us (99%)
  local copies, waits for them, and re-layouts  0.69 us (1%)
    pallas_call x1, Pallas kernels, body(): pl.pallas_call(functools.partial(kernel, nc), out_shape=vmem((rows, width...  66.6 us

profile of v3, /device:TPU:1, one launch (start us, length us, event | category | flops | bytes accessed | tf_op | source)
XLA Modules:
  0.0 67.3 jit_solution(3208646728095074688)
XLA Ops:
  0.0 66.6 %shard_map.17 = f32[64,896]{1,0:T(8,128)S(1)} custom-call(f32[64,896]{1,0:T(8,128)} %x_hbm.1), custom_call_target="tpu_custom_call" | custom-call | tf_op jit(solution)/shard_map/pallas_call | solution.py:502
  66.6 0.7 %copy.3 = f32[64,896]{1,0:T(8,128)} copy(f32[64,896]{1,0:T(8,128)S(1)} %shard_map.17) | data formatting | bytes 458752

commit v4 on v3

--- a/solution.py
+++ b/solution.py
@@ -84,7 +84,7 @@
 
 def kernel(
     nc, x_hbm, out_ref,
-    xv, xz, xy, xhi, xlo, jhi, jlo, gp, gr, gs, gy, gj, tt, tz, thi, tlo, cp, cr, pp, qy, qk, pthi, ptlo, op, ry,
+    xv, xz, xy, xhi, xlo, jhi, jlo, gp, gr, gs, gy, gj, tt, tz, thi, tlo, cp, cr, pp, qy, qk, wq, pthi, ptlo, op, ry,
     sq, sqx, sqz, sqy,
     x_s, xz_s, xz_r, xy_s, xy_r, g_s, g_r, gy_s, gy_r, tz_s, tz_r, c_s, c_r, u_s, u_r, v_s, v_r, p_s, p_r, qk_s, qk_r, ry_s, ry_r,
     qx_s, qx_r, qz_s, qz_r, qy_s, qy_r,
@@ -380,16 +380,31 @@
     drain_c(7, NZ, (4,))
     from_all.append(to_all(1, 7, NZ))
     rows_to_y(2, 7, NZ)
+
+    def gather_q(part):
+        blocks = range(4 * part, 4 * part + 4)
+        for pos in blocks:
+            qk[place(0, pos), :] = pp[pos, x, core]
+        for arrive in k_waits[1:] if part else k_waits[:1]:
+            arrive()
+        for slot in range(1, NY):
+            for pos in blocks:
+                qk[place(slot, pos), :] = qy[slot - 1, pos]
+
+    def squares_early():
+        gather_q(0)
+        wq[...] = dot3((thi[:, :lanes], tlo[:, :lanes]), split(qk[:lanes, :]), 1, 0)
     u_all.wait_recv()
     to_twin.start()
     for half_t in range(2):
         every = tz.at[half_t, pl.ds(0, NZ - 1)]
         t_copy(half_t, 0, every, every).wait_send()
 
-    cut = width - 256
+    cut = 512
     parts = (pl.ds(0, cut), pl.ds(cut, width - cut))
     most = NZ // 2
     early = most * rows
+    squares_early()
     from_twin.wait_recv()
     known = jnp.concatenate([pp[:most].reshape(early, wide), jnp.zeros((NZ * rows - early, wide), F32)], axis=0)
     hi, lo = split(known.T)
@@ -431,14 +446,8 @@
             pass_on(way, 2, 1, h, c)
 
     def squares_here():
-        for pos in range(NZ):
-            qk[place(0, pos), :] = pp[pos, x, core]
-        for arrive in k_waits:
-            arrive()
-        for slot in range(1, NY):
-            for pos in range(NZ):
-                qk[place(slot, pos), :] = qy[slot - 1, pos]
-        block = dot3((thi[...], tlo[...]), split(qk[...]), 1, 0)
+        gather_q(1)
+        block = wq[...] + dot3((thi[:, lanes:], tlo[:, lanes:]), split(qk[lanes:, :]), 1, 0)
         block = block * pp[...].reshape(NZ * rows, wide)
         columns = jnp.sum(block.reshape(NZ * rows // 8, 8, wide), axis=0)
         total = columns[:, :128]
@@ -477,11 +486,11 @@
 
     u_all.wait_send()
     to_twin.wait_send()
-    arrived(1, 0)
-    arrived(1, 1)
-    for h in range(2):
-        total = op[y, halves(h), :] + (ry[0, 2 - h, :, :] + ry[1, 1 + h, :, :])
-        out_ref[halves(h), :] = factor * total
+    for c in range(2):
+        arrived(1, c)
+        for h in range(2):
+            total = op[y, halves(h), parts[c]] + (ry[0, 2 - h, :, parts[c]] + ry[1, 1 + h, :, parts[c]])
+            out_ref[halves(h), parts[c]] = factor * total
     for c in range(2):
         every = ry.at[:, :, :, parts[c]]
         copy(every, every, ry_s.at[c], ry_r.at[0, c], at_y(1)).wait_send()
@@ -526,6 +535,7 @@
             vmem((NZ, nc // 2, 2, sub, wide), F32),
             vmem((NY - 1, NZ, sub, wide), F32),
             vmem((owned, wide), F32),
+            vmem((NZ * rows, wide), F32),
             vmem((wide, NZ * rows), BF16),
             vmem((wide, NZ * rows), BF16),
             vmem((NY, rows, width), F32),

time: 67.4 us -> 66.9 us (level)
  no operation moved by 1% of the time
where the time goes in v4:
time: 66.9 us
  Pallas kernels  66.2 us (99%)
  local copies, waits for them, and re-layouts  0.69 us (1%)
    pallas_call x1, Pallas kernels, body(): pl.pallas_call(functools.partial(kernel, nc), out_shape=vmem((rows, width...  66.2 us

profile of v4, /device:TPU:1, one launch (start us, length us, event | category | flops | bytes accessed | tf_op | source)
XLA Modules:
  0.0 66.9 jit_solution(12027407304681505031)
XLA Ops:
  0.0 66.2 %shard_map.17 = f32[64,896]{1,0:T(8,128)S(1)} custom-call(f32[64,896]{1,0:T(8,128)} %x_hbm.1), custom_call_target="tpu_custom_call" | custom-call | tf_op jit(solution)/shard_map/pallas_call | solution.py:511
  66.2 0.7 %copy.3 = f32[64,896]{1,0:T(8,128)} copy(f32[64,896]{1,0:T(8,128)S(1)} %shard_map.17) | data formatting | bytes 458752

commit v5 on v4

--- a/solution.py
+++ b/solution.py
@@ -475,9 +475,9 @@
     total = take(0, now, total)
     now = give(1, total)
     finish(0)
-    finish(1)
     total = take(1, now, total)
     now = give(2, total)
+    finish(1)
     for done in closing[:-1]:
         done()
     total = take(2, now, total)

time: 66.9 us -> 67.1 us (level)
  no operation moved by 1% of the time
where the time goes in v5:
time: 67.1 us; the launch traced here: 67 us
  Pallas kernels  66.3 us (99%)
  local copies, waits for them, and re-layouts  0.69 us (1%)
    pallas_call x1, Pallas kernels, body(): pl.pallas_call(functools.partial(kernel, nc), out_shape=vmem((rows, width...  66.3 us

profile of v5, /device:TPU:1, one launch (start us, length us, event | category | flops | bytes accessed | tf_op | source)
XLA Modules:
  0.0 67.0 jit_solution(15128910957458304909)
XLA Ops:
  0.0 66.3 %shard_map.17 = f32[64,896]{1,0:T(8,128)S(1)} custom-call(f32[64,896]{1,0:T(8,128)} %x_hbm.1), custom_call_target="tpu_custom_call" | custom-call | tf_op jit(solution)/shard_map/pallas_call | solution.py:511
  66.3 0.7 %copy.3 = f32[64,896]{1,0:T(8,128)} copy(f32[64,896]{1,0:T(8,128)S(1)} %shard_map.17) | data formatting | bytes 458752

commit v6 on v4

--- a/solution.py
+++ b/solution.py
@@ -10,7 +10,7 @@
 N = 7168
 NY = 4
 NZ = 8
-X_PARTS = 4
+X_PARTS = 2
 
 LINEAR_TERM = 3.4445
 CUBIC_TERM = -4.775

time: 66.9 us -> 67.9 us (1.015)
  Pallas kernels: 66.2 us -> 67.1 us
    pallas_call x1, Pallas kernels: 66.2 us -> 67.1 us  [body(): pl.pallas_call(functools.partial(kernel, nc), out_shape=vmem((rows, width...]
where the time goes in v6:
time: 67.9 us; the launch traced here: 67.8 us
  Pallas kernels  67.1 us (99%)
  local copies, waits for them, and re-layouts  0.69 us (1%)
    pallas_call x1, Pallas kernels, body(): pl.pallas_call(functools.partial(kernel, nc), out_shape=vmem((rows, width...  67.1 us

profile of v6, /device:TPU:1, one launch (start us, length us, event | category | flops | bytes accessed | tf_op | source)
XLA Modules:
  0.0 67.8 jit_solution(961834817689701151)
XLA Ops:
  0.0 67.1 %shard_map.17 = f32[64,896]{1,0:T(8,128)S(1)} custom-call(f32[64,896]{1,0:T(8,128)} %x_hbm.1), custom_call_target="tpu_custom_call" | custom-call | tf_op jit(solution)/shard_map/pallas_call | solution.py:511
  67.1 0.7 %copy.3 = f32[64,896]{1,0:T(8,128)} copy(f32[64,896]{1,0:T(8,128)S(1)} %shard_map.17) | data formatting | bytes 458752
